TPU v7x, 32 devices: a whole 2x2x4 slice. The times are simulated.
32 devices in a mesh: segment: 2 (over y), fsdp: 4 (over x, core), seq: 4 (over z).
Axes of the slice: x: 2, y: 2, z: 4, core: 2. Of those that a mesh axis runs over, the one named last changes fastest.
Arguments:
- arriving: bfloat16 [2, 4, 768, 2048], P('segment', 'fsdp', 'seq'), may hold values from -6 to 6
- gain: float32 [2, 2048], P('segment'), may hold values from 0.1 to 1.9
- input_weight: bfloat16 [2, 2048, 16, 3, 128], P('segment', 'fsdp', 'seq')
- output_weight: bfloat16 [2, 16, 128, 2048], P('segment', 'seq', None, 'fsdp'), may hold values from -1 to 1
- block_pattern: int32 [2, 4, 24, 6], P('segment', 'fsdp'), may hold values from 0 to 23, as said below
Outputs:
- passed: bfloat16 [2, 4, 768, 2048], P('segment', 'fsdp', 'seq')
Inputs may be any that keep to these rules, and one draw needn't show every extreme that they name: `block_pattern`: row j of a document lists 6 different blocks; the first three are j - 1, j and j + 1 modulo 24, and block 0 is listed in every row.
All inputs are finite; a program needn't handle non-finite values.
Results may differ from a plain program's by a relative error of at most 0.012.
Values may be sent and summed in bfloat16 or wider, within the bound.
A program may use at most 64 MiB of HBM per device.

v0:
```python
import jax
import jax.numpy as jnp
from jax import lax
from jax.sharding import PartitionSpec as P

BLOCK = 32
SEL = 6
EPSILON = 1e-05


def passed_along(value, axis, steps):
    count = lax.axis_size(axis)
    pairs = [(source, (source + steps) % count) for source in range(count)]
    return lax.ppermute(value, axis, pairs)


def normalize(tokens, gain_row):
    values = tokens.astype(jnp.float32)
    spread = jnp.mean(values * values, axis=-1, keepdims=True)
    return (values * lax.rsqrt(spread + EPSILON) * gain_row).astype(jnp.bfloat16)


def attend(projected, pattern_rows):
    length, head_group, triple, head_width = projected.shape
    block_count = length // BLOCK
    query_rows = projected[:, :, 0].reshape(block_count, BLOCK, head_group, head_width)
    key_blocks = projected[:, :, 1].reshape(block_count, BLOCK, head_group, head_width)
    value_blocks = projected[:, :, 2].reshape(block_count, BLOCK, head_group, head_width)
    key_rows = jnp.take(key_blocks, pattern_rows, axis=0).reshape(
        block_count, SEL * BLOCK, head_group, head_width
    )
    value_rows = jnp.take(value_blocks, pattern_rows, axis=0).reshape(
        block_count, SEL * BLOCK, head_group, head_width
    )
    scores = jnp.einsum(
        "qbge,qnge->gqbn", query_rows, key_rows, preferred_element_type=jnp.float32
    ) * head_width ** (-0.5)
    row_max = jnp.max(scores, axis=-1, keepdims=True)
    exponent = jnp.exp(scores - row_max)
    weights = (exponent / jnp.sum(exponent, axis=-1, keepdims=True)).astype(jnp.bfloat16)
    mixed_rows = jnp.einsum(
        "gqbn,qnge->qbge", weights, value_rows, preferred_element_type=jnp.float32
    )
    return mixed_rows.astype(jnp.bfloat16).reshape(length, head_group * head_width)


def body(arriving, gain, input_weight, output_weight, block_pattern):
    tokens = arriving[0, 0]
    row_count = tokens.shape[0]
    normed = normalize(tokens, gain[0])
    slab_rows, head_group, triple, head_size = input_weight.shape[1:]
    columns = head_group * triple * head_size
    panel_flat = input_weight[0].reshape(slab_rows, columns)
    length = row_count * lax.axis_size("seq")
    whole_panel = lax.all_gather(panel_flat, "fsdp", axis=0, tiled=True)
    projected = jnp.dot(
        lax.all_gather(normed, "seq", axis=0, tiled=True),
        whole_panel,
        preferred_element_type=jnp.float32,
    )
    projected = projected.astype(jnp.bfloat16).reshape(length, head_group, triple, head_size)
    mixed_rows = attend(projected, block_pattern[0, 0])
    out_panel = output_weight[0].reshape(head_group * head_size, -1)
    whole_out = lax.all_gather(out_panel, "fsdp", axis=1, tiled=True)
    branch = lax.psum_scatter(
        jnp.dot(mixed_rows, whole_out, preferred_element_type=jnp.float32).astype(jnp.bfloat16),
        "seq",
        scatter_dimension=0,
        tiled=True,
    ).astype(jnp.float32)
    updated = (tokens.astype(jnp.float32) + branch).astype(jnp.bfloat16)
    passed = passed_along(updated, "segment", 1)
    return passed[None, None]


def solution(mesh):
    in_specs = (
        P("segment", "fsdp", "seq", None),
        P("segment", None),
        P("segment", "fsdp", "seq", None, None),
        P("segment", "seq", None, "fsdp"),
        P("segment", "fsdp", None, None),
    )
    out_specs = P("segment", "fsdp", "seq", None)
    return jax.shard_map(body, mesh=mesh, in_specs=in_specs, out_specs=out_specs, check_vma=False)
```

profile of v0, /device:TPU:0, one launch (start us, length us, event | category | flops | bytes accessed | tf_op | source)
XLA Modules:
  0.0 277.0 jit_solution(2608817675597869169)
XLA Ops:
  6.5 1.5 fusion.4
  8.0 2.3 fusion.6
  10.3 0.0 all-gather.6.cloned.1.call-start
  10.4 2.6 copy.24
  13.0 0.0 all-gather.8.cloned.1.call-start
  13.0 0.7 all-gather.8.cloned.1.call-update
  13.7 0.0 reduce-scatter.2.cloned.1.call-start
  13.8 0.1 copy.27
  13.9 0.1 reshape.54
  14.0 0.1 copy.23
  14.1 62.6 %all-gather.4.cloned.1.call-done = bf16[768,2048]{1,0:T(8,128)(2,1)} async-done(((bf16[192,2048]{1,0:T(8,128)(2,1)}), bf16[768,2048]{1,0:T(8,128)(2,1)}) %all-gather.4.cloned.1.call-update) | async-done | bytes 3145744 | tf_op jit(solution)/shard_map/all_gather | solution.py:57
  76.7 46.6 %all-gather.6.cloned.1.call-done = bf16[2048,1536]{0,1:T(8,128)(2,1)} async-done(((bf16[512,1536]{0,1:T(8,128)(2,1)}), bf16[2048,1536]{0,1:T(8,128)(2,1)}) %all-gather.6.cloned.1.call-update) | async-done | bytes 6291472 | tf_op jit(solution)/shard_map/all_gather | solution.py:55
  123.3 9.3 %convolution_convert_fusion.1 = bf16[768,1536]{1,0:T(8,128)(2,1)} fusion(bf16[768,2048]{1,0:T(8,128)(2,1)} %all-gather.4.cloned.1.call-done, bf16[2048,1536]{0,1:T(8,128)(2,1)} %all-gather.6.cloned.1.call-done), kind=kOutput, calls=%fused_computation.6 | convolution fusion | flops 4833017856 | bytes 11796480 | tf_op jit(solution)/shard_map/dot_general | solution.py:56
  132.6 2.9 %copy.25 = bf16[768,1536]{0,1:T(8,128)(2,1)S(1)} copy(bf16[768,1536]{1,0:T(8,128)(2,1)} %convolution_convert_fusion.1) | data formatting | bytes 4718592 | tf_op jit(solution)/shard_map/convert_element_type | solution.py:61
  135.5 1.3 fusion.20
  136.8 1.5 copy.31
  138.3 1.5 copy.26
  139.8 7.6 %gather_fusion.1 = bf16[144,32,4,128]{3,1,2,0:T(8,128)(2,1)} fusion(bf16[24,32,4,128]{3,1,0,2:T(8,128)(2,1)S(1)} %bitcast.37, s32[1024]{0:T(1024)S(1)} %pad_clamp_fusion), kind=kCustom, calls=%fused_computation.1.clone | custom fusion | bytes 9437760 | tf_op jit(solution)/shard_map/jit(_take)/gather | solution.py:29
  147.4 7.6 %gather_fusion = bf16[144,32,4,128]{3,1,2,0:T(8,128)(2,1)} fusion(bf16[24,32,4,128]{3,1,0,2:T(8,128)(2,1)S(1)} %bitcast.36, s32[1024]{0:T(1024)S(1)} %pad_clamp_fusion), kind=kCustom, calls=%fused_computation.clone | custom fusion | bytes 9437760 | tf_op jit(solution)/shard_map/jit(_take)/gather | solution.py:32
  155.0 5.7 %broadcast_select_fusion = (bf16[24,6,32,4,128]{4,2,3,1,0:T(8,128)(2,1)S(1)}, bf16[24,6,32,4,128]{4,2,3,1,0:T(8,128)(2,1)}) fusion(bf16[24,6,32,4,128]{4,2,3,1,0:T(8,128)(2,1)} %bitcast.38, pred[24,6]{1,0:T(8,128)(4,1)S(1)} %copy.23, bf16[24,6,32,4,128]{4,2,3,1,0:T(8,128)(2,1)} %bitcast.39), kind=kLoop, calls=%fused_computation.3 | loop fusion | flops 4718592 | bytes 18874512 | tf_op jit(solution)/shard_map/jit(_take)/select_n | solution.py:29
  160.7 3.6 %copy.33 = bf16[24,6,32,4,128]{4,2,1,0,3:T(8,128)(2,1)} copy(bf16[24,6,32,4,128]{4,2,3,1,0:T(8,128)(2,1)S(1)} %get-tuple-element.9) | data formatting | bytes 9437184 | tf_op jit(solution)/shard_map/jit(_take)/select_n | solution.py:29
  164.2 0.4 copy.29
  164.6 5.9 %copy.28 = bf16[24,6,32,4,128]{4,2,1,3,0:T(8,128)(2,1)} copy(bf16[24,6,32,4,128]{4,2,3,1,0:T(8,128)(2,1)} %get-tuple-element.10) | data formatting | bytes 9437184 | tf_op jit(solution)/shard_map/jit(_take)/select_n | solution.py:32
  170.5 7.2 %fusion.21 = (f32[4,24,32]{2,1,0:T(8,128)S(1)}, f32[4,24,32,192]{3,2,1,0:T(8,128)}) fusion(bf16[24,32,4,128]{3,1,0,2:T(8,128)(2,1)S(1)} %bitcast.44, bf16[24,192,4,128]{3,1,0,2:T(8,128)(2,1)} %bitcast.40), kind=kOutput, calls=%fused_computation.31 | convolution fusion | flops 152764608 | bytes 7876608 | tf_op jit(solution)/shard_map/sub | solution.py:39
  177.7 5.2 %fusion.14 = bf16[24,32,4,128]{3,1,2,0:T(8,128)(2,1)S(1)} fusion(bf16[24,192,4,128]{3,1,2,0:T(8,128)(2,1)} %bitcast.43, f32[4,24,32,192]{3,2,1,0:T(8,128)} %get-tuple-element.12, f32[4,24,32]{2,1,0:T(8,128)S(1)} %get-tuple-element.11), kind=kOutput, calls=%fused_computation.22 | convolution fusion | flops 152567808 | bytes 7876608 | tf_op jit(solution)/shard_map/gqbn,qnge->qbge/dot_general | solution.py:41
  182.9 0.4 copy.35
  183.3 5.0 %convolution_convert_fusion = bf16[768,2048]{1,0:T(8,128)(2,1)} fusion(bf16[512,2048]{1,0:T(8,128)(2,1)} %all-gather.8.cloned.1.call-done, bf16[96,8,4,128]{3,2,1,0:T(4,128)(2,1)S(1)} %bitcast.45), kind=kOutput, calls=%fused_computation.5 | convolution fusion | flops 1612185600 | bytes 6029312 | tf_op jit(solution)/shard_map/dot_general | solution.py:66
  188.4 60.6 %reduce-scatter.2.cloned.1.call-done = bf16[192,2048]{1,0:T(8,128)(2,1)} async-done(((bf16[768,2048]{1,0:T(8,128)(2,1)}), bf16[192,2048]{1,0:T(8,128)(2,1)}) %reduce-scatter.2.cloned.1.call-update) | async-done | bytes 786448 | tf_op jit(solution)/shard_map/reduce_scatter | solution.py:65
  248.9 1.4 fusion.7
  250.4 1.5 collective-permute-start
  251.9 17.7 %collective-permute-done = bf16[192,2048]{1,0:T(8,128)(2,1)S(1)} collective-permute-done((bf16[192,2048]{1,0:T(8,128)(2,1)S(1)}, bf16[192,2048]{1,0:T(8,128)(2,1)S(1)}, u32[]{:S(2)}, u32[]{:S(2)}) %collective-permute-start) | collective-permute-done | bytes 786464 | tf_op jit(solution)/shard_map/ppermute | solution.py:14
  269.5 0.9 copy.52
  (15 shorter events, 0.1 us)
Async XLA Ops:
  6.5 3.8 %copy-start.1 = (bf16[1,512,4,3,128]{4,2,3,1,0:T(4,128)(2,1)S(1)}, bf16[1,512,4,3,128]{4,2,3,1,0:T(4,128)(2,1)}, u32[]{:S(2)}) copy-start(bf16[1,512,4,3,128]{4,2,3,1,0:T(4,128)(2,1)} %param.9) | copy-start | bytes 4718596
  6.5 70.1 %all-gather.4.cloned.1.call-start = ((), (), s32[]{:S(2)}) async-start(), calls=%async_computation.1 | async-start | bytes 3932160 | tf_op jit(solution)/shard_map/all_gather | solution.py:57
  10.3 3.5 %copy-start.2 = (s32[1,1,24,6]{2,1,3,0:T(1,128)S(1)}, s32[1,1,24,6]{2,1,3,0:T(1,128)}, u32[]{:S(2)}) copy-start(s32[1,1,24,6]{2,1,3,0:T(1,128)} %param.11) | copy-start | bytes 1732
  10.3 113.0 %all-gather.6.cloned.1.call-start = ((), (), s32[]{:S(2)}) async-start(), calls=%async_computation.2 | async-start | bytes 7864320 | tf_op jit(solution)/shard_map/all_gather | solution.py:55
  13.0 170.3 %all-gather.8.cloned.1.call-start = ((), (), s32[]{:S(2)}) async-start(), calls=%async_computation.3 | async-start | bytes 2621440 | tf_op jit(solution)/shard_map/all_gather | solution.py:64
  13.7 235.2 %reduce-scatter.2.cloned.1.call-start = ((), (), s32[]{:S(2)}) async-start(), calls=%async_computation.4 | async-start | bytes 3932160 | tf_op jit(solution)/shard_map/reduce_scatter | solution.py:65
  188.3 60.6 %copy-start = (bf16[1,1,192,2048]{3,2,1,0:T(8,128)(2,1)S(1)}, bf16[1,1,192,2048]{3,2,1,0:T(8,128)(2,1)}, u32[]{:S(2)}) copy-start(bf16[1,1,192,2048]{3,2,1,0:T(8,128)(2,1)} %param.7) | copy-start | bytes 2359300
  250.4 19.2 %collective-permute-start = (bf16[192,2048]{1,0:T(8,128)(2,1)S(1)}, bf16[192,2048]{1,0:T(8,128)(2,1)S(1)}, u32[]{:S(2)}, u32[]{:S(2)}) collective-permute-start(bf16[192,2048]{1,0:T(8,128)(2,1)S(1)} %fusion.7), channel_id=1, source_target_pairs={{0,16},{16,0},{1,17},{17,1},{2,18},{18,2},{3,19},{19,3},{4,20},{20... | collective-permute-start | bytes 2359304 | tf_op jit(solution)/shard_map/ppermute | solution.py:14
Sparse Core Ops, SparseCore 0:
  10.5 66.1 all-gather.3
  78.2 45.0 all-gather.5
  124.9 22.5 all-gather.7
  188.5 60.4 reduce-scatter.1
where the time goes:
time: 277 us
  waiting for transfers between devices  188 us (68%)
  local copies, waits for them, and re-layouts  36.4 us (13%)
  matrix products  26.7 us (10%)
  between operations  13.2 us (5%)
  other arithmetic  10.8 us (4%)
    all_gather x1, waiting for transfers between devices, body(): lax.all_gather(normed, 'seq', axis=0, tiled=True)  62.6 us
    reduce_scatter x1, waiting for transfers between devices, body(): lax.psum_scatter(jnp.dot(mixed_rows, whole_out, preferred_element_type=jn...  60.6 us
    all_gather x1, waiting for transfers between devices, body(): whole_panel = lax.all_gather(panel_flat, 'fsdp', axis=0, tiled=True)  46.6 us
    ppermute x1, waiting for transfers between devices, passed_along(): return lax.ppermute(value, axis, pairs)  17.7 us
    dot_general x1, matrix products, body(): jnp.dot(lax.all_gather(normed, 'seq', axis=0, tiled=True), whole_panel, p...  9.27 us
    gather x1, local copies, waits for them, and re-layouts, attend(): jnp.take(value_blocks, pattern_rows, axis=0)  7.62 us
    gather x1, local copies, waits for them, and re-layouts, attend(): jnp.take(key_blocks, pattern_rows, axis=0)  7.56 us
    sub x1, matrix products, attend(): exponent = jnp.exp(scores - row_max)  7.16 us
  transfers between devices with their start and end apart: 5, of which 4 were waited for; matrix products, arithmetic and copies ran while one was open for 23% of the time, Pallas kernels for 0%

commit v1 on v0

--- a/solution.py
+++ b/solution.py
@@ -6,6 +6,27 @@
 BLOCK = 32
 SEL = 6
 EPSILON = 1e-05
+
+
+def ring_gather(x, axis, dim):
+    size, position, rows = (lax.axis_size(axis), lax.axis_index(axis), x.shape[dim])
+    right = [(i, (i + 1) % size) for i in range(size)]
+    behind = [(i, (i - 1) % size) for i in range(size)]
+    out = jnp.zeros((*x.shape[:dim], size * rows, *x.shape[dim + 1 :]), x.dtype)
+    out = lax.dynamic_update_slice_in_dim(out, x, position * rows, axis=dim)
+    from_left = from_right = x
+    halfway = size // 2
+    for hop in range(1, halfway + 1):
+        from_left = lax.ppermute(from_left, axis, right)
+        out = lax.dynamic_update_slice_in_dim(
+            out, from_left, (position - hop) % size * rows, axis=dim
+        )
+        if hop < size - halfway:
+            from_right = lax.ppermute(from_right, axis, behind)
+            out = lax.dynamic_update_slice_in_dim(
+                out, from_right, (position + hop) % size * rows, axis=dim
+            )
+    return out
 
 
 def passed_along(value, axis, steps):
@@ -54,9 +75,7 @@
     length = row_count * lax.axis_size("seq")
     whole_panel = lax.all_gather(panel_flat, "fsdp", axis=0, tiled=True)
     projected = jnp.dot(
-        lax.all_gather(normed, "seq", axis=0, tiled=True),
-        whole_panel,
-        preferred_element_type=jnp.float32,
+        ring_gather(normed, "seq", 0), whole_panel, preferred_element_type=jnp.float32
     )
     projected = projected.astype(jnp.bfloat16).reshape(length, head_group, triple, head_size)
     mixed_rows = attend(projected, block_pattern[0, 0])

time: 277 us -> 225 us (0.81)
  waiting for transfers between devices: 188 us -> 126 us
  local copies, waits for them, and re-layouts: 36.4 us -> 42.8 us
  starting transfers between devices: 1.66 us -> 6.75 us
    all_gather x1 -> x0, waiting for transfers between devices: 62.6 us -> none  [body(): lax.all_gather(normed, 'seq', axis=0, tiled=True)]
    ppermute x0 -> x3, waiting for transfers between devices: none -> 49.1 us  [the longest x2 34.8 us: ring_gather(): from_left = lax.ppermute(from_left, axis, right)]
    all_gather x1, waiting for transfers between devices: 46.6 us -> 0.01 us  [body(): whole_panel = lax.all_gather(panel_flat, 'fsdp', axis=0, tiled=True)]
    ppermute x0 -> x3, starting transfers between devices: none -> 5.13 us  [the longest x2 3.02 us: ring_gather(): from_left = lax.ppermute(from_left, axis, right)]
    dynamic_update_slice x0 -> x3, local copies, waits for them, and re-layouts: none -> 2.99 us  [the longest x2 2.05 us: ring_gather(): lax.dynamic_update_slice_in_dim(out, from_left, (position - hop) % size *...]
  transfers between devices with their start and end apart: 5 -> 7, of which waited for: 4 -> 5; matrix products, arithmetic and copies ran while one was open for 23% -> 30% of each run, Pallas kernels for 0% -> 0%
where the time goes in v1:
time: 225 us
  waiting for transfers between devices  126 us (56%)
  local copies, waits for them, and re-layouts  42.8 us (19%)
  matrix products  26.6 us (12%)
  between operations  13.3 us (6%)
  other arithmetic  8.73 us (4%)
  starting transfers between devices  6.75 us (3%)
    reduce_scatter x1, waiting for transfers between devices, body(): lax.psum_scatter(jnp.dot(mixed_rows, whole_out, preferred_element_type=jn...  59.6 us
    ppermute x2, waiting for transfers between devices, ring_gather(): from_left = lax.ppermute(from_left, axis, right)  34.8 us
    ppermute x1, waiting for transfers between devices, passed_along(): return lax.ppermute(value, axis, pairs)  17.7 us
    ppermute x1, waiting for transfers between devices, ring_gather(): from_right = lax.ppermute(from_right, axis, behind)  14.3 us
    dot_general x1, matrix products, body(): jnp.dot(ring_gather(normed, 'seq', 0), whole_panel, preferred_element_typ...  9.24 us
    gather x1, local copies, waits for them, and re-layouts, attend(): jnp.take(value_blocks, pattern_rows, axis=0)  7.61 us
    gather x1, local copies, waits for them, and re-layouts, attend(): jnp.take(key_blocks, pattern_rows, axis=0)  7.57 us
    sub x1, matrix products, attend(): exponent = jnp.exp(scores - row_max)  7.15 us
  transfers between devices with their start and end apart: 7, of which 5 were waited for; matrix products, arithmetic and copies ran while one was open for 30% of the time, Pallas kernels for 0%

profile of v1, /device:TPU:0, one launch (start us, length us, event | category | flops | bytes accessed | tf_op | source)
XLA Modules:
  0.0 224.6 jit_solution(13464098414395343134)
XLA Ops:
  6.5 3.8 %copy.24 = bf16[1,512,4,3,128]{1,4,3,2,0:T(8,128)(2,1)} copy(bf16[1,512,4,3,128]{4,2,3,1,0:T(4,128)(2,1)} %param.9) | data formatting | bytes 3145728 | tf_op args[2]
  10.5 0.2 fusion.4
  10.7 2.1 broadcast_in_dim.18
  12.8 1.4 constant_dynamic-update-slice_fusion.3
  14.2 3.0 %collective-permute-start = (bf16[192,2048]{1,0:T(8,128)(2,1)}, bf16[192,2048]{1,0:T(8,128)(2,1)S(1)}, u32[]{:S(2)}, u32[]{:S(2)}) collective-permute-start(bf16[192,2048]{1,0:T(8,128)(2,1)} %get-tuple-element.7), channel_id=1, source_target_pairs={{0,1},{1,2},{2,3},{3,0},{4,5},{5,6},{6,7},{7,4},{8,9},{9,10},{10,1... | collective-permute-start | bytes 2359304 | tf_op jit(solution)/shard_map/ppermute | solution.py:20
  17.2 2.1 collective-permute-start.1
  19.7 18.3 %collective-permute-done = bf16[192,2048]{1,0:T(8,128)(2,1)S(1)} collective-permute-done((bf16[192,2048]{1,0:T(8,128)(2,1)}, bf16[192,2048]{1,0:T(8,128)(2,1)S(1)}, u32[]{:S(2)}, u32[]{:S(2)}) %collective-permute-start) | collective-permute-done | bytes 786464 | tf_op jit(solution)/shard_map/ppermute | solution.py:20
  38.1 1.0 constant_dynamic-update-slice_fusion.2
  39.1 14.3 %collective-permute-done.1 = bf16[192,2048]{1,0:T(8,128)(2,1)S(1)} collective-permute-done((bf16[192,2048]{1,0:T(8,128)(2,1)}, bf16[192,2048]{1,0:T(8,128)(2,1)S(1)}, u32[]{:S(2)}, u32[]{:S(2)}) %collective-permute-start.1) | collective-permute-done | bytes 786464 | tf_op jit(solution)/shard_map/ppermute | solution.py:25
  53.4 0.9 constant_dynamic-update-slice_fusion.1
  54.4 16.5 %collective-permute-done.2 = bf16[192,2048]{1,0:T(8,128)(2,1)S(1)} collective-permute-done((bf16[192,2048]{1,0:T(8,128)(2,1)S(1)}, bf16[192,2048]{1,0:T(8,128)(2,1)S(1)}, u32[]{:S(2)}, u32[]{:S(2)}) %collective-permute-start.2) | collective-permute-done | bytes 786464 | tf_op jit(solution)/shard_map/ppermute | solution.py:20
  70.8 1.0 constant_dynamic-update-slice_fusion
  71.9 9.2 %convolution_convert_fusion.1 = bf16[768,1536]{1,0:T(8,128)(2,1)} fusion(bf16[768,2048]{1,0:T(8,128)(2,1)} %constant_dynamic-update-slice_fusion, bf16[2048,1536]{0,1:T(8,128)(2,1)} %all-gather.3.cloned.1.call-done), kind=kOutput, calls=%fused_computation.6 | convolution fusion | flops 4833017856 | bytes 11796480 | tf_op jit(solution)/shard_map/dot_general | solution.py:77
  81.1 2.9 %copy.25 = bf16[768,1536]{0,1:T(8,128)(2,1)S(1)} copy(bf16[768,1536]{1,0:T(8,128)(2,1)} %convolution_convert_fusion.1) | data formatting | bytes 4718592 | tf_op jit(solution)/shard_map/convert_element_type | solution.py:80
  84.0 1.5 fusion.21
  85.4 1.5 copy.31
  86.9 1.5 copy.26
  88.4 7.6 %gather_fusion.1 = bf16[144,32,4,128]{3,1,2,0:T(8,128)(2,1)} fusion(bf16[24,32,4,128]{3,1,0,2:T(8,128)(2,1)S(1)} %bitcast.38, s32[1024]{0:T(1024)S(1)} %pad_clamp_fusion), kind=kCustom, calls=%fused_computation.1.clone | custom fusion | bytes 9437760 | tf_op jit(solution)/shard_map/jit(_take)/gather | solution.py:50
  96.0 7.6 %gather_fusion = bf16[144,32,4,128]{3,1,2,0:T(8,128)(2,1)} fusion(bf16[24,32,4,128]{3,1,0,2:T(8,128)(2,1)S(1)} %bitcast.37, s32[1024]{0:T(1024)S(1)} %pad_clamp_fusion), kind=kCustom, calls=%fused_computation.clone | custom fusion | bytes 9437760 | tf_op jit(solution)/shard_map/jit(_take)/gather | solution.py:53
  103.6 5.7 %broadcast_select_fusion = (bf16[24,6,32,4,128]{4,2,3,1,0:T(8,128)(2,1)S(1)}, bf16[24,6,32,4,128]{4,2,3,1,0:T(8,128)(2,1)}) fusion(bf16[24,6,32,4,128]{4,2,3,1,0:T(8,128)(2,1)} %bitcast.39, pred[24,6]{1,0:T(8,128)(4,1)S(1)} %copy.23, bf16[24,6,32,4,128]{4,2,3,1,0:T(8,128)(2,1)} %bitcast.40), kind=kLoop, calls=%fused_computation.3 | loop fusion | flops 4718592 | bytes 18874512 | tf_op jit(solution)/shard_map/jit(_take)/select_n | solution.py:50
  109.3 3.5 %copy.33 = bf16[24,6,32,4,128]{4,2,1,0,3:T(8,128)(2,1)} copy(bf16[24,6,32,4,128]{4,2,3,1,0:T(8,128)(2,1)S(1)} %get-tuple-element.11) | data formatting | bytes 9437184 | tf_op jit(solution)/shard_map/jit(_take)/select_n | solution.py:50
  112.8 0.4 copy.29
  113.2 6.0 %copy.28 = bf16[24,6,32,4,128]{4,2,1,3,0:T(8,128)(2,1)} copy(bf16[24,6,32,4,128]{4,2,3,1,0:T(8,128)(2,1)} %get-tuple-element.12) | data formatting | bytes 9437184 | tf_op jit(solution)/shard_map/jit(_take)/select_n | solution.py:53
  119.1 7.2 %fusion.22 = (f32[4,24,32]{2,1,0:T(8,128)S(1)}, f32[4,24,32,192]{3,2,1,0:T(8,128)}) fusion(bf16[24,32,4,128]{3,1,0,2:T(8,128)(2,1)S(1)} %bitcast.45, bf16[24,192,4,128]{3,1,0,2:T(8,128)(2,1)} %bitcast.41), kind=kOutput, calls=%fused_computation.35 | convolution fusion | flops 152764608 | bytes 7876608 | tf_op jit(solution)/shard_map/sub | solution.py:60
  126.3 5.2 %fusion.14 = bf16[24,32,4,128]{3,1,2,0:T(8,128)(2,1)S(1)} fusion(bf16[24,192,4,128]{3,1,2,0:T(8,128)(2,1)} %bitcast.44, f32[4,24,32,192]{3,2,1,0:T(8,128)} %get-tuple-element.14, f32[4,24,32]{2,1,0:T(8,128)S(1)} %get-tuple-element.13), kind=kOutput, calls=%fused_computation.22 | convolution fusion | flops 152567808 | bytes 7876608 | tf_op jit(solution)/shard_map/gqbn,qnge->qbge/dot_general | solution.py:62
  131.5 0.4 copy.35
  131.9 5.0 %convolution_convert_fusion = bf16[768,2048]{1,0:T(8,128)(2,1)} fusion(bf16[512,2048]{1,0:T(8,128)(2,1)} %all-gather.5.cloned.1.call-done, bf16[96,8,4,128]{3,2,1,0:T(4,128)(2,1)S(1)} %bitcast.46), kind=kOutput, calls=%fused_computation.5 | convolution fusion | flops 1612185600 | bytes 6029312 | tf_op jit(solution)/shard_map/dot_general | solution.py:85
  137.0 59.6 %reduce-scatter.2.cloned.1.call-done = bf16[192,2048]{1,0:T(8,128)(2,1)} async-done(((bf16[768,2048]{1,0:T(8,128)(2,1)}), bf16[192,2048]{1,0:T(8,128)(2,1)}) %reduce-scatter.2.cloned.1.call-update) | async-done | bytes 786448 | tf_op jit(solution)/shard_map/reduce_scatter | solution.py:84
  196.6 1.4 fusion.7
  198.0 1.5 collective-permute-start.3
  199.5 17.7 %collective-permute-done.3 = bf16[192,2048]{1,0:T(8,128)(2,1)S(1)} collective-permute-done((bf16[192,2048]{1,0:T(8,128)(2,1)S(1)}, bf16[192,2048]{1,0:T(8,128)(2,1)S(1)}, u32[]{:S(2)}, u32[]{:S(2)}) %collective-permute-start.3) | collective-permute-done | bytes 786464 | tf_op jit(solution)/shard_map/ppermute | solution.py:35
  217.2 0.9 copy.56
  (24 shorter events, 0.5 us)
Async XLA Ops:
  6.5 3.9 %copy-start = (bf16[1,1,192,2048]{3,2,1,0:T(8,128)(2,1)S(1)}, bf16[1,1,192,2048]{3,2,1,0:T(8,128)(2,1)}, u32[]{:S(2)}) copy-start(bf16[1,1,192,2048]{3,2,1,0:T(8,128)(2,1)} %param.7) | copy-start | bytes 2359300
  6.5 65.3 %all-gather.3.cloned.1.call-start = ((), (), s32[]{:S(2)}) async-start(), calls=%async_computation.1 | async-start | bytes 7864320 | tf_op jit(solution)/shard_map/all_gather | solution.py:76
  10.4 2.4 %copy-start.3 = (f32[1,2048]{1,0:T(1,128)S(1)}, f32[1,2048]{1,0:T(1,128)}, u32[]{:S(2)}) copy-start(f32[1,2048]{1,0:T(1,128)} %param.8) | copy-start | bytes 24580
  10.4 121.5 %all-gather.5.cloned.1.call-start = ((), (), s32[]{:S(2)}) async-start(), calls=%async_computation.2 | async-start | bytes 2621440 | tf_op jit(solution)/shard_map/all_gather | solution.py:83
  10.7 8.8 %copy-start.2 = (s32[1,1,24,6]{2,1,3,0:T(1,128)S(1)}, s32[1,1,24,6]{2,1,3,0:T(1,128)}, u32[]{:S(2)}) copy-start(s32[1,1,24,6]{2,1,3,0:T(1,128)} %param.11) | copy-start | bytes 1732
  14.2 23.8 %collective-permute-start = (bf16[192,2048]{1,0:T(8,128)(2,1)}, bf16[192,2048]{1,0:T(8,128)(2,1)S(1)}, u32[]{:S(2)}, u32[]{:S(2)}) collective-permute-start(bf16[192,2048]{1,0:T(8,128)(2,1)} %get-tuple-element.7), channel_id=1, source_target_pairs={{0,1},{1,2},{2,3},{3,0},{4,5},{5,6},{6,7},{7,4},{8,9},{9,10},{10,1... | collective-permute-start | bytes 2359304 | tf_op jit(solution)/shard_map/ppermute | solution.py:20
  17.2 36.2 %collective-permute-start.1 = (bf16[192,2048]{1,0:T(8,128)(2,1)}, bf16[192,2048]{1,0:T(8,128)(2,1)S(1)}, u32[]{:S(2)}, u32[]{:S(2)}) collective-permute-start(bf16[192,2048]{1,0:T(8,128)(2,1)} %get-tuple-element.7), channel_id=1, source_target_pairs={{0,3},{1,0},{2,1},{3,2},{4,7},{5,4},{6,5},{7,6},{8,11},{9,8},{10,9... | collective-permute-start | bytes 2359304 | tf_op jit(solution)/shard_map/ppermute | solution.py:25
  19.4 177.2 %reduce-scatter.2.cloned.1.call-start = ((), (), s32[]{:S(2)}) async-start(), calls=%async_computation.3 | async-start | bytes 3932160 | tf_op jit(solution)/shard_map/reduce_scatter | solution.py:84
  38.0 32.9 %collective-permute-start.2 = (bf16[192,2048]{1,0:T(8,128)(2,1)S(1)}, bf16[192,2048]{1,0:T(8,128)(2,1)S(1)}, u32[]{:S(2)}, u32[]{:S(2)}) collective-permute-start(bf16[192,2048]{1,0:T(8,128)(2,1)S(1)} %collective-permute-done), channel_id=1, source_target_pairs={{0,1},{1,2},{2,3},{3,0},{4,5},{5,6},{6,7},{7,4},{8,9},{9,10},{10,1... | collective-permute-start | bytes 2359304 | tf_op jit(solution)/shard_map/ppermute | solution.py:20
  109.3 3.5 %copy-start.1 = (bf16[768,4,1,128]{0,3,2,1:T(8,128)(2,1)S(1)}, bf16[768,4,1,128]{0,3,2,1:T(8,128)(2,1)}, u32[]{:S(2)}) copy-start(bf16[768,4,1,128]{0,3,2,1:T(8,128)(2,1)} %get-tuple-element.9) | copy-start | bytes 2359300
  198.0 19.2 %collective-permute-start.3 = (bf16[192,2048]{1,0:T(8,128)(2,1)S(1)}, bf16[192,2048]{1,0:T(8,128)(2,1)S(1)}, u32[]{:S(2)}, u32[]{:S(2)}) collective-permute-start(bf16[192,2048]{1,0:T(8,128)(2,1)S(1)} %fusion.7), channel_id=1, source_target_pairs={{0,16},{16,0},{1,17},{17,1},{2,18},{18,2},{3,19},{19,3},{4,20},{20... | collective-permute-start | bytes 2359304 | tf_op jit(solution)/shard_map/ppermute | solution.py:35
Sparse Core Ops, SparseCore 0:
  10.5 49.0 all-gather.2
  61.2 22.5 all-gather.4
  137.1 59.4 reduce-scatter.1
